TPU v7x, 32 devices: a whole 2x2x4 slice. The times are simulated.
32 devices in a mesh: prow: 4 (over y, core), pcol: 8 (over z, x).
Axes of the slice: x: 2, y: 2, z: 4, core: 2. Of those that a mesh axis runs over, the one named last changes fastest.
Arguments:
- matrix: float32 [10240, 9216], P('prow', 'pcol'), as said below
- pivots: int32 [1024], replicated, may hold values from 0 to 10239, as said below
Outputs:
- updated: float32 [10240, 9216], P('prow', 'pcol')
Inputs may be any that keep to these rules, and one draw needn't show every extreme that they name: For each i < 1024, pivots[i] is i or a row index of 1024 or more; indices of 1024 or more are distinct. `matrix`: the first 1024 columns hold the factored panel: below the diagonal, the multipliers of the lower factor.
All inputs are finite; a program needn't handle non-finite values.
Results may differ from a plain program's by a relative error of at most 0.000051.
Values sent between devices are 32-bit elements; how exact they have to be, the bound alone decides.
A program may use at most 128 MiB of HBM per device.

v0:
```python
import jax
import jax.numpy as jnp
from jax import lax
from jax.sharding import PartitionSpec as P


def spread(block, axis, owner):
    block = jnp.where(lax.axis_index(axis) == owner, block, jnp.zeros_like(block))
    return lax.psum(block, axis)


def on_device(matrix, pivots):
    row_count = matrix.shape[0]
    col_count = matrix.shape[1]
    panel_width = pivots.shape[0]
    prow_index = lax.axis_index("prow")
    pcol_index = lax.axis_index("pcol")
    panel_rows = spread(matrix[:, :panel_width], "pcol", 0)
    pieces = ((panel_rows, 0, panel_width),)
    owner_prow = pivots // row_count
    local_row = pivots - owner_prow * row_count
    is_mine = (owner_prow == prow_index)[:, None]
    contribution = jnp.where(is_mine, matrix[local_row], 0.0)
    new_top = lax.psum(contribution, "prow")
    old_top = spread(matrix[:panel_width], "prow", 0)

    def solve_top(top_rows):
        return lax.linalg.triangular_solve(
            panel_rows[:panel_width], top_rows, left_side=True, lower=True, unit_diagonal=True
        )

    solved = lax.cond(prow_index == 0, solve_top, jnp.zeros_like, new_top)
    upper_rows = spread(solved, "prow", 0)
    destination = jnp.where(
        (owner_prow == prow_index) & (pivots >= panel_width), local_row, row_count
    )
    swapped = matrix.at[destination].set(old_top, mode="drop")
    piece, begin, finish = pieces[0]
    product = jnp.dot(
        piece, upper_rows, precision=lax.Precision.HIGHEST, preferred_element_type=jnp.float32
    )
    result = swapped - product
    padded_upper = jnp.concatenate(
        [upper_rows, jnp.zeros((row_count - panel_width, col_count), jnp.float32)], axis=0
    )
    global_row = prow_index * row_count + lax.broadcasted_iota(jnp.int32, (row_count, 1), 0)
    result = jnp.where(global_row < panel_width, padded_upper, result)
    global_col = pcol_index * col_count + lax.broadcasted_iota(jnp.int32, (1, col_count), 1)
    return jnp.where(global_col < panel_width, matrix, result)


def solution(mesh):
    return jax.shard_map(
        on_device,
        mesh=mesh,
        in_specs=(P("prow", "pcol"), P()),
        out_specs=P("prow", "pcol"),
        check_vma=False,
    )
```

profile of v0, /device:TPU:0, one launch (start us, length us, event | category | flops | bytes accessed | tf_op | source)
XLA Modules:
  0.0 838.4 jit_solution(6654059166047416843)
XLA Ops:
  6.5 0.0 all-reduce.8.cloned.1.call-start
  6.5 0.7 fusion.35
  7.2 0.7 broadcast_compare_fusion
  7.9 11.0 %gather_fusion = f32[1024,1152]{1,0:T(8,128)} fusion(f32[2560,1152]{1,0:T(8,128)} %param.4, s32[1024]{0:T(1024)S(1)} %get-tuple-element.63), kind=kCustom, calls=%fused_computation | custom fusion | bytes 9441280 | tf_op jit(solution)/shard_map/gather | solution.py:23
  19.0 4.8 broadcast_select_fusion.1
  23.8 0.0 all-reduce.8.cloned.1.call-update
  23.8 0.0 all-reduce.6.cloned.1.call-start
  23.9 10.8 %slice_select_fusion = f32[2560,1024]{1,0:T(8,128)} fusion(f32[2560,1152]{1,0:T(8,128)} %param.4, pred[]{:T(512)S(6)} %eq.17), kind=kLoop, calls=%fused_computation.86 | loop fusion | flops 2621440 | bytes 20971520 | tf_op jit(solution)/shard_map/jit(_where)/select_n | solution.py:8
  34.7 0.0 all-reduce.6.cloned.1.call-update
  34.7 0.0 all-reduce.10.cloned.1.call-start
  34.7 4.8 slice_select_fusion.1
  39.6 81.1 %all-reduce.8.cloned.1.call-done = f32[1024,1152]{1,0:T(8,128)} async-done(((f32[1024,1152]{1,0:T(8,128)}), f32[1024,1152]{1,0:T(8,128)}) %all-reduce.8.cloned.1.call-update) | async-done | bytes 4718608 | tf_op jit(solution)/shard_map/psum | solution.py:24
  120.7 331.4 %all-reduce.6.cloned.1.call-done = f32[2560,1024]{1,0:T(8,128)} async-done(((f32[2560,1024]{1,0:T(8,128)}), f32[2560,1024]{1,0:T(8,128)}) %all-reduce.6.cloned.1.call-update) | async-done | bytes 10485776 | tf_op jit(solution)/shard_map/psum | solution.py:9
  452.1 138.6 %conditional.1 = (f32[1024,1152]{1,0:T(8,128)}) conditional(s32[]{:T(128)} %convert_element_type.3, () %tuple.11, (f32[2560,1024]{1,0:T(8,128)}, f32[1024,1152]{1,0:T(8,128)}) %tuple.12), branch_computations={%region_2.3_spmd, %region_3.4_spmd} | conditional | flops 8162952192 | bytes 76947776 | solution.py:32
  452.1 4.6 convert_add_fusion
  456.7 23.3 %while.1 = (s32[]{:T(128)}, f32[1024,1024]{1,0:T(8,128)}, s32[8,2]{0,1:T(2,128)S(1)}, f32[8,128,128]{2,1,0:T(8,128)S(1)}, s32[]{:T(128)}) while((s32[]{:T(128)}, f32[1024,1024]{1,0:T(8,128)}, s32[8,2]{0,1:T(2,128)S(1)}, f32[8,128,128]{2,1,0:T(8,128)S(1)}, s32[]{:T(128)}) %tuple.50), condition=%wide.while_cond, body=%wide.while_body.sunk | while | flops 2 | bytes 131181 | solution.py:28
  456.7 0.1 constant_dynamic-slice_fusion.2
  456.7 0.6 fusion.52
  457.3 2.2 bitcast_dynamic-update-slice_fusion.2
  459.6 0.1 constant_dynamic-slice_fusion.2
  459.7 0.6 fusion.52
  460.3 2.2 bitcast_dynamic-update-slice_fusion.2
  462.5 0.1 constant_dynamic-slice_fusion.2
  462.6 0.6 fusion.52
  463.2 2.2 bitcast_dynamic-update-slice_fusion.2
  465.5 0.1 constant_dynamic-slice_fusion.2
  465.5 0.6 fusion.52
  466.1 2.2 bitcast_dynamic-update-slice_fusion.2
  468.4 0.1 constant_dynamic-slice_fusion.2
  468.5 0.6 fusion.52
  469.1 2.2 bitcast_dynamic-update-slice_fusion.2
  471.3 0.1 constant_dynamic-slice_fusion.2
  471.4 0.6 fusion.52
  472.0 2.2 bitcast_dynamic-update-slice_fusion.2
  474.2 0.1 constant_dynamic-slice_fusion.2
  474.3 0.6 fusion.52
  474.9 2.2 bitcast_dynamic-update-slice_fusion.2
  477.2 0.1 constant_dynamic-slice_fusion.2
  477.2 0.6 fusion.52
  477.8 2.2 bitcast_dynamic-update-slice_fusion.2
  480.0 78.8 %custom-call.2 = f32[8,128,128]{1,2,0:T(8,128)S(1)} custom-call(f32[8,128,128]{2,1,0:T(8,128)S(1)} %get-tuple-element.21), custom_call_target="InvertDiagBlocksLowerTriangular" | custom-call | tf_op jit(solution)/shard_map/cond/branch_1_fun/triangular_solve | solution.py:28
  558.8 0.0 copy-start
  558.8 2.8 constant_dynamic-update-slice_fusion.17
  561.6 1.7 convolution_subtract_fusion.6
  563.3 1.6 constant_dynamic-update-slice_fusion.16
  565.0 0.0 copy-done
  565.0 1.7 convolution_subtract_fusion.5
  566.7 1.6 constant_dynamic-update-slice_fusion.15
  568.3 2.2 convolution_subtract_fusion.2
  570.5 1.6 constant_dynamic-update-slice_fusion.14
  572.1 2.4 convolution_subtract_fusion.4
  574.6 1.5 constant_dynamic-update-slice_fusion.13
  576.1 3.0 convolution_subtract_fusion
  579.1 1.5 constant_dynamic-update-slice_fusion.12
  580.6 3.4 convolution_subtract_fusion.1
  584.0 1.5 constant_dynamic-update-slice_fusion.11
  585.5 3.7 convolution_subtract_fusion.3
  589.2 1.5 convolution_dynamic-update-slice_fusion
  590.7 4.8 broadcast_select_fusion
  595.5 0.0 all-reduce.10.cloned.1.call-update
  595.5 10.4 %copy.38 = f32[2560,1152]{1,0:T(8,128)} copy(f32[2560,1152]{1,0:T(8,128)} %param.4) | data formatting | bytes 23592960
  605.9 158.1 %all-reduce.10.cloned.1.call-done = (f32[1024,1152]{1,0:T(8,128)}, f32[1024,1152]{1,0:T(8,128)}) async-done(((f32[1024,1152]{1,0:T(8,128)}, f32[1024,1152]{1,0:T(8,128)}), (f32[1024,1152]{1,0:T(8,128)}, f32[1024,1152]{1,0:T(8,128)})) %all-reduce.10.cloned.1.call-update) | async-done | bytes 9437200 | tf_op jit(solution)/shard_map/psum | solution.py:9
  763.9 15.0 %scatter_fusion = f32[2560,1152]{1,0:T(8,128)} fusion(f32[2560,1152]{1,0:T(8,128)} %copy.38, s32[1024]{0:T(1024)S(1)} %get-tuple-element.64, f32[1024,1152]{1,0:T(8,128)} %get-tuple-element.30), kind=kCustom, calls=%fused_computation.1 | custom fusion | bytes 14159872 | tf_op jit(solution)/shard_map/scatter | solution.py:37
  778.9 53.0 %fusion.34 = f32[2560,1152]{1,0:T(8,128)} fusion(f32[2560,1152]{1,0:T(8,128)} %param.4, f32[2560,1152]{1,0:T(8,128)} %scatter_fusion, f32[2560,1024]{1,0:T(8,128)} %all-reduce.6.cloned.1.call-done, f32[1024,1152]{1,0:T(8,128)} %get-tuple-element.31, pred[2560]{0:T(1024)(128)(4,1)S(1)} %add_compare_fusion, pred[1152]{0:T(1024)(128)(4,1)S(1)} %add_compare_fusion.1), kind=kOutput, calls=%fused_computation.85 | convolution fusion | flops 36247633920 | bytes 50597504 | tf_op jit(solution)/shard_map/dot_general | solution.py:39
  (6 shorter events, 0.0 us)
Async XLA Ops:
  6.5 114.2 %all-reduce.8.cloned.1.call-start = ((), (), s32[]{:S(2)}) async-start(), calls=%async_computation.1 | async-start | bytes 9437184 | tf_op jit(solution)/shard_map/psum | solution.py:24
  23.8 428.3 %all-reduce.6.cloned.1.call-start = ((), (), s32[]{:S(2)}) async-start(), calls=%async_computation | async-start | bytes 20971520 | tf_op jit(solution)/shard_map/psum | solution.py:9
  34.7 729.3 %all-reduce.10.cloned.1.call-start = ((), (), s32[]{:S(2)}) async-start(), calls=%async_computation.2 | async-start | bytes 18874368 | tf_op jit(solution)/shard_map/psum | solution.py:9
  558.8 6.2 copy-start
Sparse Core Ops, SparseCore 0:
  23.9 96.7 all-reduce.7
  124.6 327.4 all-reduce.5
  595.6 168.2 all-reduce.9
where the time goes:
time: 839 us; the launch traced here: 838 us
  waiting for transfers between devices  571 us (68%)
  other arithmetic  110 us (13%)
  matrix products  84.9 us (10%)
  local copies, waits for them, and re-layouts  59.5 us (7%)
  between operations  13.1 us (2%)
    psum x2, waiting for transfers between devices, spread(): return lax.psum(block, axis)  489 us
    another operation x4, other arithmetic, solve_top(): lax.linalg.triangular_solve(panel_rows[:panel_width], top_rows, left_side...  83.4 us
    psum x1, waiting for transfers between devices, on_device(): new_top = lax.psum(contribution, 'prow')  81.1 us
    dot_general x1, matrix products, on_device(): jnp.dot(piece, upper_rows, precision=lax.Precision.HIGHEST, preferred_ele...  53 us
    another operation x15, matrix products, solve_top(): lax.linalg.triangular_solve(panel_rows[:panel_width], top_rows, left_side...  31.9 us
    another operation x24, local copies, waits for them, and re-layouts  23.2 us
    select_n x3, other arithmetic, spread(): jnp.where(lax.axis_index(axis) == owner, block, jnp.zeros_like(block))  20.4 us
  transfers between devices with their start and end apart: 3, of which 3 were waited for; matrix products, arithmetic and copies ran while one was open for 3% of the time, Pallas kernels for 0%

commit v1 on v0

--- a/solution.py
+++ b/solution.py
@@ -21,7 +21,8 @@
     local_row = pivots - owner_prow * row_count
     is_mine = (owner_prow == prow_index)[:, None]
     contribution = jnp.where(is_mine, matrix[local_row], 0.0)
-    new_top = lax.psum(contribution, "prow")
+    parts = lax.all_gather(contribution, "prow")
+    new_top = jnp.sum(parts, axis=0)
     old_top = spread(matrix[:panel_width], "prow", 0)
 
     def solve_top(top_rows):

time: 839 us -> 762 us (0.908)
  waiting for transfers between devices: 571 us -> 473 us
  other arithmetic: 110 us -> 122 us
    psum x2, waiting for transfers between devices: 489 us -> 367 us  [spread(): return lax.psum(block, axis)]
    all_gather x0 -> x1, waiting for transfers between devices: none -> 106 us  [on_device(): parts = lax.all_gather(contribution, 'prow')]
    psum x1 -> x0, waiting for transfers between devices: 81.1 us -> none  [on_device(): new_top = lax.psum(contribution, 'prow')]
    reduce_sum x0 -> x1, other arithmetic: none -> 10.2 us  [on_device(): new_top = jnp.sum(parts, axis=0)]
  transfers between devices with their start and end apart: 3 -> 3, of which waited for: 3 -> 3; matrix products, arithmetic and copies ran while one was open for 3% -> 5% of each run, Pallas kernels for 0% -> 0%
where the time goes in v1:
time: 762 us; the launch traced here: 755 us
  waiting for transfers between devices  473 us (62%)
  other arithmetic  122 us (16%)
  matrix products  85.2 us (11%)
  local copies, waits for them, and re-layouts  59.5 us (8%)
  between operations  15.1 us (2%)
    psum x2, waiting for transfers between devices, spread(): return lax.psum(block, axis)  367 us
    all_gather x1, waiting for transfers between devices, on_device(): parts = lax.all_gather(contribution, 'prow')  106 us
    another operation x4, other arithmetic, solve_top(): lax.linalg.triangular_solve(panel_rows[:panel_width], top_rows, left_side...  83.4 us
    dot_general x1, matrix products, on_device(): jnp.dot(piece, upper_rows, precision=lax.Precision.HIGHEST, preferred_ele...  53.1 us
    another operation x15, matrix products, solve_top(): lax.linalg.triangular_solve(panel_rows[:panel_width], top_rows, left_side...  32.1 us
    another operation x24, local copies, waits for them, and re-layouts  23 us
    select_n x3, other arithmetic, spread(): jnp.where(lax.axis_index(axis) == owner, block, jnp.zeros_like(block))  21.9 us
  transfers between devices with their start and end apart: 3, of which 3 were waited for; matrix products, arithmetic and copies ran while one was open for 5% of the time, Pallas kernels for 0%

profile of v1, /device:TPU:0, one launch (start us, length us, event | category | flops | bytes accessed | tf_op | source)
XLA Modules:
  0.0 754.9 jit_solution(2111273828710288298)
XLA Ops:
  7.4 0.0 all-gather.2.cloned.1.call-start
  7.4 0.7 fusion.35
  8.1 0.7 broadcast_compare_fusion
  8.8 11.0 %gather_fusion = f32[1024,1152]{1,0:T(8,128)} fusion(f32[2560,1152]{1,0:T(8,128)} %param.4, s32[1024]{0:T(1024)S(1)} %get-tuple-element.63), kind=kCustom, calls=%fused_computation | custom fusion | bytes 9441280 | tf_op jit(solution)/shard_map/gather | solution.py:23
  19.8 5.0 bitcast_select_fusion
  24.8 0.0 all-gather.2.cloned.1.call-update
  24.8 0.0 all-reduce.5.cloned.1.call-start
  24.8 11.2 %slice_select_fusion = f32[2560,1024]{1,0:T(8,128)} fusion(f32[2560,1152]{1,0:T(8,128)} %param.4, pred[]{:T(512)S(6)} %eq.17), kind=kLoop, calls=%fused_computation.86 | loop fusion | flops 2621440 | bytes 20971520 | tf_op jit(solution)/shard_map/jit(_where)/select_n | solution.py:8
  36.1 0.0 all-reduce.5.cloned.1.call-update
  36.1 0.0 all-reduce.7.cloned.1.call-start
  36.2 5.8 slice_select_fusion.1
  42.0 105.7 %all-gather.2.cloned.1.call-done = f32[4,1024,1152]{2,1,0:T(8,128)} async-done(((f32[1,1024,1152]{2,1,0:T(8,128)}), f32[4,1024,1152]{2,1,0:T(8,128)}) %all-gather.2.cloned.1.call-update) | async-done | bytes 18874384 | tf_op jit(solution)/shard_map/all_gather | solution.py:24
  147.7 10.2 %reduce_sum.9 = f32[1024,1152]{1,0:T(8,128)} reduce(f32[4,1024,1152]{2,1,0:T(8,128)} %all-gather.2.cloned.1.call-done, f32[]{:T(128)} %constant.41.clone.1), dimensions={0}, to_apply=%region_1.2 | reduce | flops 3538944 | bytes 23592964 | tf_op jit(solution)/shard_map/reduce_sum | solution.py:25
  157.9 208.8 %all-reduce.5.cloned.1.call-done = f32[2560,1024]{1,0:T(8,128)} async-done(((f32[2560,1024]{1,0:T(8,128)}), f32[2560,1024]{1,0:T(8,128)}) %all-reduce.5.cloned.1.call-update) | async-done | bytes 10485776 | tf_op jit(solution)/shard_map/psum | solution.py:9
  366.6 139.0 %conditional.1 = (f32[1024,1152]{1,0:T(8,128)}) conditional(s32[]{:T(128)} %convert_element_type.3, () %tuple.11, (f32[2560,1024]{1,0:T(8,128)}, f32[1024,1152]{1,0:T(8,128)}) %tuple.12), branch_computations={%region_2.3_spmd, %region_3.4_spmd} | conditional | flops 8162952192 | bytes 76947776 | solution.py:33
  366.6 4.5 convert_add_fusion
  371.2 23.2 %while.1 = (s32[]{:T(128)}, f32[1024,1024]{1,0:T(8,128)}, s32[8,2]{0,1:T(2,128)S(1)}, f32[8,128,128]{2,1,0:T(8,128)S(1)}, s32[]{:T(128)}) while((s32[]{:T(128)}, f32[1024,1024]{1,0:T(8,128)}, s32[8,2]{0,1:T(2,128)S(1)}, f32[8,128,128]{2,1,0:T(8,128)S(1)}, s32[]{:T(128)}) %tuple.50), condition=%wide.while_cond, body=%wide.while_body.sunk | while | flops 2 | bytes 131181 | solution.py:29
  371.2 0.1 constant_dynamic-slice_fusion.2
  371.2 0.6 fusion.52
  371.8 2.2 bitcast_dynamic-update-slice_fusion.2
  374.1 0.1 constant_dynamic-slice_fusion.2
  374.1 0.6 fusion.52
  374.7 2.2 bitcast_dynamic-update-slice_fusion.2
  377.0 0.1 constant_dynamic-slice_fusion.2
  377.1 0.6 fusion.52
  377.6 2.2 bitcast_dynamic-update-slice_fusion.2
  379.9 0.1 constant_dynamic-slice_fusion.2
  380.0 0.6 fusion.52
  380.5 2.2 bitcast_dynamic-update-slice_fusion.2
  382.8 0.1 constant_dynamic-slice_fusion.2
  382.9 0.6 fusion.52
  383.5 2.2 bitcast_dynamic-update-slice_fusion.2
  385.7 0.1 constant_dynamic-slice_fusion.2
  385.8 0.6 fusion.52
  386.4 2.2 bitcast_dynamic-update-slice_fusion.2
  388.6 0.1 constant_dynamic-slice_fusion.2
  388.7 0.6 fusion.52
  389.3 2.2 bitcast_dynamic-update-slice_fusion.2
  391.5 0.1 constant_dynamic-slice_fusion.2
  391.6 0.6 fusion.52
  392.2 2.2 bitcast_dynamic-update-slice_fusion.2
  394.3 78.9 %custom-call.2 = f32[8,128,128]{1,2,0:T(8,128)S(1)} custom-call(f32[8,128,128]{2,1,0:T(8,128)S(1)} %get-tuple-element.21), custom_call_target="InvertDiagBlocksLowerTriangular" | custom-call | tf_op jit(solution)/shard_map/cond/branch_1_fun/triangular_solve | solution.py:29
  473.2 0.0 copy-start
  473.3 2.8 constant_dynamic-update-slice_fusion.17
  476.1 1.7 convolution_subtract_fusion.6
  477.8 1.6 constant_dynamic-update-slice_fusion.16
  479.4 1.7 convolution_subtract_fusion.5
  481.1 1.6 constant_dynamic-update-slice_fusion.15
  482.7 2.2 convolution_subtract_fusion.2
  485.0 1.6 constant_dynamic-update-slice_fusion.14
  486.6 2.4 convolution_subtract_fusion.4
  489.0 1.5 constant_dynamic-update-slice_fusion.13
  490.6 3.0 convolution_subtract_fusion
  493.5 1.5 constant_dynamic-update-slice_fusion.12
  495.0 3.7 convolution_subtract_fusion.1
  498.8 1.5 constant_dynamic-update-slice_fusion.11
  500.3 3.7 convolution_subtract_fusion.3
  503.9 1.5 convolution_dynamic-update-slice_fusion
  505.6 4.9 broadcast_select_fusion
  510.5 0.0 all-reduce.7.cloned.1.call-update
  510.5 10.3 %copy.37 = f32[2560,1152]{1,0:T(8,128)} copy(f32[2560,1152]{1,0:T(8,128)} %param.4) | data formatting | bytes 23592960
  520.9 158.1 %all-reduce.7.cloned.1.call-done = (f32[1024,1152]{1,0:T(8,128)}, f32[1024,1152]{1,0:T(8,128)}) async-done(((f32[1024,1152]{1,0:T(8,128)}, f32[1024,1152]{1,0:T(8,128)}), (f32[1024,1152]{1,0:T(8,128)}, f32[1024,1152]{1,0:T(8,128)})) %all-reduce.7.cloned.1.call-update) | async-done | bytes 9437200 | tf_op jit(solution)/shard_map/psum | solution.py:9
  679.0 15.1 %scatter_fusion = f32[2560,1152]{1,0:T(8,128)} fusion(f32[2560,1152]{1,0:T(8,128)} %copy.37, s32[1024]{0:T(1024)S(1)} %get-tuple-element.64, f32[1024,1152]{1,0:T(8,128)} %get-tuple-element.30), kind=kCustom, calls=%fused_computation.1 | custom fusion | bytes 14159872 | tf_op jit(solution)/shard_map/scatter | solution.py:38
  694.1 53.1 %fusion.34 = f32[2560,1152]{1,0:T(8,128)} fusion(f32[2560,1152]{1,0:T(8,128)} %param.4, f32[2560,1152]{1,0:T(8,128)} %scatter_fusion, f32[2560,1024]{1,0:T(8,128)} %all-reduce.5.cloned.1.call-done, f32[1024,1152]{1,0:T(8,128)} %get-tuple-element.31, pred[2560]{0:T(1024)(128)(4,1)S(1)} %add_compare_fusion, pred[1152]{0:T(1024)(128)(4,1)S(1)} %add_compare_fusion.1), kind=kOutput, calls=%fused_computation.85 | convolution fusion | flops 36247633920 | bytes 50597504 | tf_op jit(solution)/shard_map/dot_general | solution.py:40
  (7 shorter events, 0.0 us)
Async XLA Ops:
  7.4 140.3 %all-gather.2.cloned.1.call-start = ((), (), s32[]{:S(2)}) async-start(), calls=%async_computation.1 | async-start | bytes 23592960 | tf_op jit(solution)/shard_map/all_gather | solution.py:24
  24.8 341.8 %all-reduce.5.cloned.1.call-start = ((), (), s32[]{:S(2)}) async-start(), calls=%async_computation | async-start | bytes 20971520 | tf_op jit(solution)/shard_map/psum | solution.py:9
  36.1 642.9 %all-reduce.7.cloned.1.call-start = ((), (), s32[]{:S(2)}) async-start(), calls=%async_computation.2 | async-start | bytes 18874368 | tf_op jit(solution)/shard_map/psum | solution.py:9
  473.2 6.1 copy-start
Sparse Core Ops, SparseCore 0:
  24.9 122.7 all-gather.1
  510.6 168.3 all-reduce.6
Sparse Core Ops, SparseCore 1:
  36.2 330.4 all-reduce.4
